TPU v7x, 32 devices: a whole 2x2x4 slice. The times are simulated.
32 devices in a mesh: state: 8 (over z, x), basis: 4 (over y, core).
Axes of the slice: x: 2, y: 2, z: 4, core: 2. Of those that a mesh axis runs over, the one named last changes fastest.
Arguments:
- lower_vectors: bfloat16 [61440, 3072], P('basis', 'state'), may hold values from -6 to 6
- upper_vectors: bfloat16 [61440, 2048], P('basis', 'state'), may hold values from -6 to 6
- lower_labels: int32 [3072], P('state'), may hold values from 0 to 3
- upper_labels: int32 [2048], P('state'), may hold values from 0 to 3
- band_offsets: int32 [960], P('basis'), may hold values from -2 to 2
- dipole_blocks: bfloat16 [960, 64, 128], P('basis'), may hold values from -0.5 to 0.5
- pair_table: int32 [4, 4], replicated, may hold values 0 or 1
Outputs:
- moments: float32 [3072, 1024], P('state', 'basis')
All inputs are finite; a program needn't handle non-finite values.
Results may differ from a plain program's by a relative error of at most 0.0029.
Values may be sent and summed in bfloat16 or wider, within the bound.
A program may use at most 128 MiB of HBM per device.

v0:
```python
import jax
import jax.numpy as jnp
from jax import lax
from jax.sharding import PartitionSpec as P

STEPS = 4


def with_halo(block, sides, width):
    for axis, dim in sides:
        count = lax.axis_size(axis)
        forward = [(i, i + 1) for i in range(count - 1)]
        backward = [(target, source) for source, target in forward]
        low = lax.ppermute(
            lax.slice_in_dim(block, block.shape[dim] - width, None, axis=dim), axis, forward
        )
        high = lax.ppermute(lax.slice_in_dim(block, 0, width, axis=dim), axis, backward)
        block = jnp.concatenate([low, block, high], axis=dim)
    return block


def shifted(value, axis, steps):
    count = lax.axis_size(axis)
    pairs = [(source, (source + steps) % count) for source in range(count)]
    return lax.ppermute(value, axis, pairs)


def pair_term(lower_vectors, lower_onehot, table_values, norm_scale, received):
    image_part, label_part = received
    symbols = jnp.arange(table_values.shape[0], dtype=jnp.int32)
    upper_onehot = (label_part[:, None] == symbols[None, :]).astype(jnp.float32)
    allowed = jnp.dot(
        jnp.dot(lower_onehot, table_values, precision=lax.Precision.HIGHEST),
        upper_onehot.T,
        precision=lax.Precision.HIGHEST,
    )
    product = lax.dot_general(
        lower_vectors, image_part, (((0,), (0,)), ((), ())), preferred_element_type=jnp.float32
    )
    return product * allowed * norm_scale


def local(
    lower_vectors,
    upper_vectors,
    lower_labels,
    upper_labels,
    band_offsets,
    dipole_blocks,
    pair_table,
):
    block_count = dipole_blocks.shape[0]
    block_size = dipole_blocks.shape[1]
    upper_count = upper_vectors.shape[1]
    lower_count = lower_vectors.shape[1]
    padded = with_halo(upper_vectors, (("basis", 0),), 2 * block_size)
    blocks = padded.reshape(block_count + 4, block_size, upper_count)
    own_blocks = blocks[2 : block_count + 2]
    source_rows = jnp.arange(block_count, dtype=jnp.int32) + 2 + band_offsets
    coupled = jnp.take(blocks, source_rows, axis=0)
    stacked = jnp.concatenate([own_blocks, coupled], axis=1)
    dipole_image = jnp.einsum(
        "kij,kjn->kin", dipole_blocks, stacked, preferred_element_type=jnp.float32
    )
    dipole_image = dipole_image.astype(jnp.bfloat16).reshape(block_count * block_size, upper_count)
    total_rows = lower_vectors.shape[0] * lax.axis_size("basis")
    norm_scale = float(total_rows) ** (-0.5)
    table_values = pair_table.astype(jnp.float32)
    symbols = jnp.arange(pair_table.shape[0], dtype=jnp.int32)
    lower_onehot = (lower_labels[:, None] == symbols[None, :]).astype(jnp.float32)
    carried = (dipole_image, upper_labels)
    settled = [pair_term(lower_vectors, lower_onehot, table_values, norm_scale, carried)]
    for cycle_step in range(1, STEPS):
        carried = shifted((carried[0], carried[1]), "state", 1)
        settled.append(pair_term(lower_vectors, lower_onehot, table_values, norm_scale, carried))
    stacked_terms = jnp.stack(settled, axis=2).reshape(lower_count, upper_count * STEPS)
    return lax.psum_scatter(stacked_terms, "basis", scatter_dimension=1, tiled=True)


def solution(mesh):
    return jax.shard_map(
        local,
        mesh=mesh,
        in_specs=(
            P("basis", "state"),
            P("basis", "state"),
            P("state"),
            P("state"),
            P("basis"),
            P("basis", None, None),
            P(),
        ),
        out_specs=P("state", "basis"),
        check_vma=False,
    )
```

profile of v0, /device:TPU:0, one launch (start us, length us, event | category | flops | bytes accessed | tf_op | source)
XLA Modules:
  0.0 662.8 jit_solution(4209013775430671281)
XLA Ops:
  6.5 0.0 reduce-scatter.2.cloned.1.call-start
  6.5 0.9 fusion.29
  7.4 2.4 collective-permute-start
  9.8 1.3 collective-permute-start.1
  11.1 0.7 compare_and_fusion
  11.8 0.0 collective-permute-done
  11.8 3.3 collective-permute-done.1
  15.1 17.7 %pad_maximum_fusion = bf16[15616,256]{1,0:T(8,128)(2,1)} fusion(bf16[128,256]{1,0:T(8,128)(2,1)S(1)} %collective-permute-done.1, bf16[15360,256]{1,0:T(8,128)(2,1)} %param.8, bf16[128,256]{1,0:T(8,128)(2,1)S(1)} %collective-permute-done), kind=kLoop, calls=%fused_computation.5 | loop fusion | flops 23986176 | bytes 15990784 | tf_op jit(solution)/shard_map/concatenate | solution.py:18
  32.8 11.8 %gather_fusion = bf16[240,64,256]{2,1,0:T(8,128)(2,1)} fusion(bf16[244,64,256]{2,1,0:T(8,128)(2,1)} %bitcast.56, s32[1024]{0:T(1024)S(1)} %pad_clamp_fusion), kind=kCustom, calls=%fused_computation | custom fusion | bytes 15729600 | tf_op jit(solution)/shard_map/jit(_take)/gather | solution.py:60
  44.6 7.2 %broadcast_select_fusion = bf16[240,64,256]{2,1,0:T(8,128)(2,1)} fusion(bf16[240,64,256]{2,1,0:T(8,128)(2,1)} %gather_fusion, pred[240]{0:T(512)(128)(4,1)S(1)} %get-tuple-element.5), kind=kLoop, calls=%fused_computation.6 | loop fusion | flops 3932160 | bytes 15728880 | tf_op jit(solution)/shard_map/jit(_take)/select_n | solution.py:60
  51.7 0.0 copy-start
  51.7 0.0 copy-start.1
  51.7 0.0 copy-start.2
  51.7 10.8 %fusion.4 = bf16[240,256,64]{1,2,0:T(8,128)(2,1)} fusion(bf16[240,64,128]{2,1,0:T(8,128)(2,1)} %param.12, bf16[240,64,256]{2,1,0:T(8,128)(2,1)} %broadcast_select_fusion, bf16[240,64,256]{2,1,0:T(8,128)(2,1)} %bitcast.59), kind=kOutput, calls=%fused_computation.7 | convolution fusion | flops 1042022400 | bytes 27525120 | tf_op jit(solution)/shard_map/kij,kjn->kin/dot_general | solution.py:62
  62.6 1.5 collective-permute-start.2
  64.1 171.4 %collective-permute-done.2 = bf16[15360,256]{1,0:T(8,128)(2,1)S(1)} collective-permute-done((bf16[15360,256]{1,0:T(8,128)(2,1)}, bf16[15360,256]{1,0:T(8,128)(2,1)S(1)}, u32[]{:S(2)}, u32[]{:S(2)}) %collective-permute-start.2) | collective-permute-done | bytes 7864352 | tf_op jit(solution)/shard_map/ppermute | solution.py:25
  235.4 0.0 collective-permute-start.4
  235.4 173.8 %collective-permute-done.4 = bf16[15360,256]{1,0:T(8,128)(2,1)S(1)} collective-permute-done((bf16[15360,256]{1,0:T(8,128)(2,1)S(1)}, bf16[15360,256]{1,0:T(8,128)(2,1)S(1)}, u32[]{:S(2)}, u32[]{:S(2)}) %collective-permute-start.4) | collective-permute-done | bytes 7864352 | tf_op jit(solution)/shard_map/ppermute | solution.py:25
  409.3 0.0 collective-permute-start.6
  409.3 0.0 copy-done
  409.3 0.0 collective-permute-start.3
  409.3 0.0 copy-done.1
  409.3 0.0 copy-done.2
  409.3 0.3 fusion.18
  409.6 174.4 %collective-permute-done.3 = s32[256]{0:T(256)S(1)} collective-permute-done((s32[256]{0:T(256)S(1)}, s32[256]{0:T(256)S(1)}, u32[]{:S(2)}, u32[]{:S(2)}) %collective-permute-start.3) | collective-permute-done | bytes 1056 | tf_op jit(solution)/shard_map/ppermute | solution.py:25
  584.0 0.0 collective-permute-start.5
  584.0 0.4 fusion.19
  584.4 5.9 collective-permute-done.5
  590.3 0.0 collective-permute-start.7
  590.3 0.4 fusion.20
  590.6 5.9 collective-permute-done.7
  596.5 0.4 fusion.21
  596.9 0.0 slice-start
  596.9 0.0 slice-start.1
  596.9 10.9 %convolution_bitcast_fusion.3 = f32[384,256]{0,1:T(8,128)S(1)} fusion(bf16[15360,256]{1,0:T(8,128)(2,1)} %bitcast.58, bf16[15360,384]{1,0:T(8,128)(2,1)} %param.7), kind=kOutput, calls=%fused_computation.24 | convolution fusion | flops 3019898880 | bytes 20054016 | tf_op jit(solution)/shard_map/dot_general | solution.py:37
  607.9 0.4 fusion.17
  608.2 0.0 slice-start.2
  608.2 7.6 %fusion.15 = f32[384,256,1]{0,1,2:T(8,128)S(1)} fusion(f32[384,256]{0,1:T(8,128)S(1)} %fusion.19, bf16[15360,256]{1,0:T(8,128)(2,1)S(1)} %collective-permute-done.2, bf16[15360,384]{1,0:T(8,128)(2,1)} %param.7), kind=kOutput, calls=%fused_computation.20 | convolution fusion | flops 3020095488 | bytes 20447232 | tf_op jit(solution)/shard_map/dot_general | solution.py:37
  615.9 0.0 slice-done
  615.9 0.0 slice-done.1
  615.9 0.0 slice-done.2
  615.9 4.3 fusion.12
  620.2 0.0 collective-permute-done.6
  620.2 6.8 %fusion.9 = f32[384,256,1]{0,1,2:T(8,128)S(1)} fusion(f32[384,256]{0,1:T(8,128)S(1)} %fusion.21, bf16[15360,256]{1,0:T(8,128)(2,1)} %collective-permute-done.6, bf16[15360,384]{1,0:T(8,128)(2,1)S(1)} %bitcast.55), kind=kOutput, calls=%fused_computation.12 | convolution fusion | flops 3020095488 | bytes 20447232 | tf_op jit(solution)/shard_map/dot_general | solution.py:37
  627.0 0.1 pad_maximum_fusion.1
  627.1 1.0 copy.8
  628.2 1.7 reshape.22
  629.9 0.0 reduce-scatter.2.cloned.1.call-update
  629.9 24.2 %reduce-scatter.2.cloned.1.call-done = f32[384,256]{0,1:T(8,128)} async-done(((f32[384,1024]{0,1:T(8,128)}), f32[384,256]{0,1:T(8,128)}) %reduce-scatter.2.cloned.1.call-update) | async-done | bytes 393232 | tf_op jit(solution)/shard_map/reduce_scatter | solution.py:77
  654.1 1.9 copy.9
  (2 shorter events, 0.0 us)
Async XLA Ops:
  6.5 647.6 %reduce-scatter.2.cloned.1.call-start = ((), (), s32[]{:S(2)}) async-start(), calls=%async_computation.1 | async-start | bytes 1966080 | tf_op jit(solution)/shard_map/reduce_scatter | solution.py:77
  7.4 4.4 collective-permute-start
  9.8 5.3 collective-permute-start.1
  51.7 357.5 %copy-start = (s32[256]{0:T(256)S(1)}, s32[256]{0:T(256)}, u32[]{:S(2)}) copy-start(s32[256]{0:T(256)} %param.10) | copy-start | bytes 3076
  51.7 357.6 %copy-start.1 = (s32[384]{0:T(512)S(1)}, s32[384]{0:T(512)}, u32[]{:S(2)}) copy-start(s32[384]{0:T(512)} %param.9) | copy-start | bytes 4612
  51.7 357.6 %copy-start.2 = (s32[4,4]{1,0:T(4,128)S(1)}, s32[4,4]{1,0:T(4,128)}, u32[]{:S(2)}) copy-start(s32[4,4]{1,0:T(4,128)} %param.13) | copy-start | bytes 196
  62.6 172.9 %collective-permute-start.2 = (bf16[15360,256]{1,0:T(8,128)(2,1)}, bf16[15360,256]{1,0:T(8,128)(2,1)S(1)}, u32[]{:S(2)}, u32[]{:S(2)}) collective-permute-start(bf16[15360,256]{1,0:T(8,128)(2,1)} %bitcast.57), channel_id=1, source_target_pairs={{0,4},{4,8},{8,12},{12,16},{16,20},{20,24},{24,28},{28,0},{1,5},{5... | collective-permute-start | bytes 23592968 | tf_op jit(solution)/shard_map/ppermute | solution.py:25
  235.4 173.8 %collective-permute-start.4 = (bf16[15360,256]{1,0:T(8,128)(2,1)S(1)}, bf16[15360,256]{1,0:T(8,128)(2,1)S(1)}, u32[]{:S(2)}, u32[]{:S(2)}) collective-permute-start(bf16[15360,256]{1,0:T(8,128)(2,1)S(1)} %collective-permute-done.2), channel_id=1, source_target_pairs={{0,4},{4,8},{8,12},{12,16},{16,20},{20,24},{24,28},{28,0},{1,5},{5... | collective-permute-start | bytes 23592968 | tf_op jit(solution)/shard_map/ppermute | solution.py:25
  409.3 210.9 %collective-permute-start.6 = (bf16[15360,256]{1,0:T(8,128)(2,1)S(1)}, bf16[15360,256]{1,0:T(8,128)(2,1)}, u32[]{:S(2)}, u32[]{:S(2)}) collective-permute-start(bf16[15360,256]{1,0:T(8,128)(2,1)S(1)} %collective-permute-done.4), channel_id=1, source_target_pairs={{0,4},{4,8},{8,12},{12,16},{16,20},{20,24},{24,28},{28,0},{1,5},{5... | collective-permute-start | bytes 23592968 | tf_op jit(solution)/shard_map/ppermute | solution.py:25
  409.3 174.7 %collective-permute-start.3 = (s32[256]{0:T(256)S(1)}, s32[256]{0:T(256)S(1)}, u32[]{:S(2)}, u32[]{:S(2)}) collective-permute-start(s32[256]{0:T(256)S(1)} %copy-done), channel_id=1, source_target_pairs={{0,4},{4,8},{8,12},{12,16},{16,20},{20,24},{24,28},{28,0},{1,5},{5... | collective-permute-start | bytes 3080 | tf_op jit(solution)/shard_map/ppermute | solution.py:25
  584.0 6.3 collective-permute-start.5
  590.3 6.3 collective-permute-start.7
  596.9 19.0 %slice-start = ((s8[11796480]{0:T(1024)(128)(4,1)}), s8[4194304]{0:T(1024)(128)(4,1)S(1)}, s32[]{:S(2)}) async-start(s8[11796480]{0:T(1024)(128)(4,1)} %bitcast.54), calls=%async_computation.2 | async-start | bytes 8388608
  596.9 19.0 %slice-start.1 = ((s8[11796480]{0:T(1024)(128)(4,1)}), s8[4194304]{0:T(1024)(128)(4,1)S(1)}, s32[]{:S(2)}) async-start(s8[11796480]{0:T(1024)(128)(4,1)} %bitcast.54), calls=%async_computation.3 | async-start | bytes 8388608
  608.2 7.7 %slice-start.2 = ((s8[11796480]{0:T(1024)(128)(4,1)}), s8[3407872]{0:T(1024)(128)(4,1)S(1)}, s32[]{:S(2)}) async-start(s8[11796480]{0:T(1024)(128)(4,1)} %bitcast.54), calls=%async_computation.4 | async-start | bytes 6815744
Sparse Core Ops, SparseCore 0:
  630.0 24.0 reduce-scatter.1
where the time goes:
time: 663 us
  waiting for transfers between devices  559 us (84%)
  matrix products  42.2 us (6%)
  other arithmetic  25.7 us (4%)
  local copies, waits for them, and re-layouts  17.4 us (3%)
  between operations  13.6 us (2%)
    ppermute x6, waiting for transfers between devices, shifted(): return lax.ppermute(value, axis, pairs)  531 us
    dot_general x4, matrix products, pair_term(): lax.dot_general(lower_vectors, image_part, (((0,), (0,)), ((), ())), pref...  29.6 us
    reduce_scatter x1, waiting for transfers between devices, local(): lax.psum_scatter(stacked_terms, 'basis', scatter_dimension=1, tiled=True)  24.2 us
    concatenate x1, other arithmetic, with_halo(): block = jnp.concatenate([low, block, high], axis=dim)  17.7 us
  transfers between devices with their start and end apart: 9, of which 7 were waited for; matrix products, arithmetic and copies ran while one was open for 4% of the time, Pallas kernels for 0%

commit v1 on v0

v1 whole, which is shorter than its diff:
```python
import functools

import jax
import jax.numpy as jnp
from jax import lax
from jax.experimental import pallas as pl
from jax.experimental.pallas import tpu as pltpu
from jax.sharding import PartitionSpec as P

STEPS = 4
CHUNK = 512
AHEAD = 3
MESH = pl.DeviceIdType.MESH


def kernel(
    states,
    parts,
    chunks,
    block_size,
    offsets,
    low,
    high,
    upper_hbm,
    dipole,
    lower_hbm,
    out,
    upper,
    own,
    from_two,
    from_one,
    from_three,
    passing,
    lower,
    totals,
    load_sem,
    lower_sem,
    two_sem,
    one_sem,
    three_sem,
    passing_sem,
    send_up,
    send_across,
    send_swap,
    send_second,
    send_passing,
    send_last,
):
    me = lax.axis_index("state")
    odd = lax.rem(me, 2)
    is_odd = odd == 1
    is_even = odd == 0
    partner = me + 1 - 2 * odd
    above = lax.rem(me + 2, states)
    below = lax.rem(me + states - 2, states)
    blocks = upper_hbm.shape[0]
    per_chunk = CHUNK // block_size

    load = pltpu.make_async_copy(upper_hbm, upper.at[pl.ds(2, blocks)], load_sem)
    load.start()
    barrier = pltpu.get_barrier_semaphore()
    for other in (partner, above, below):
        pl.semaphore_signal(barrier, inc=1, device_id={"state": other}, device_id_type=MESH)
    upper[pl.ds(0, 2)] = low[...]
    upper[pl.ds(2 + blocks, 2)] = high[...]
    totals[...] = jnp.zeros_like(totals)
    load.wait()
    pl.semaphore_wait(barrier, 3)

    def copy(source, target, send, receive, device):
        return pltpu.make_async_remote_copy(
            src_ref=source,
            dst_ref=target,
            send_sem=send,
            recv_sem=receive,
            device_id={"state": device},
            device_id_type=MESH,
        )

    def up(c):
        return copy(own.at[c], from_two.at[c], send_up.at[c], two_sem.at[c], above)

    def across(c):
        return copy(own.at[c], from_one.at[c], send_across.at[c], one_sem.at[c], partner)

    def swap_odd(c):
        return copy(from_two.at[c], from_one.at[c], send_swap.at[c], one_sem.at[c], partner)

    def swap_even(c):
        return copy(from_two.at[c], from_three.at[c], send_swap.at[c], three_sem.at[c], partner)

    def second(c):
        return copy(from_one.at[c], from_three.at[c], send_second.at[c], three_sem.at[c], above)

    def passed(c):
        g = c // 3
        return copy(from_two.at[c], passing.at[g], send_passing.at[g], passing_sem.at[g], above)

    def last(c):
        g = c // 3
        return copy(passing.at[g], from_three.at[c], send_last.at[g], three_sem.at[c], partner)

    def make_image(c):
        for j in range(per_chunk):
            b = c * per_chunk + j
            stacked = jnp.concatenate([upper[b + 2], upper[b + 2 + offsets[b]]], axis=0)
            block = jnp.dot(dipole[b], stacked, preferred_element_type=jnp.float32)
            own[c, pl.ds(j * block_size, block_size), :] = block.astype(jnp.bfloat16)

    def body(t, carry):
        @pl.when(t < chunks)
        def _():
            make_image(t)
            up(t).start()

            @pl.when(is_even)
            def _():
                across(t).start()

        c = t - AHEAD

        @pl.when((c >= 0) & (c < chunks))
        def _():
            kind = lax.rem(c, 3)
            up(c).wait_recv()

            @pl.when(is_odd)
            def _():
                swap_odd(c).start()

            @pl.when(is_odd & (kind == 2))
            def _():
                passed(c).start()

            @pl.when(is_even & (kind != 0))
            def _():
                swap_even(c).start()

        b = t - AHEAD - 1

        @pl.when((b >= 0) & (b < chunks))
        def _():
            kind = lax.rem(b, 3)
            across(b).wait_recv()

            @pl.when((kind == 0) | (is_even & (kind == 1)))
            def _():
                second(b).start()

        e = t - AHEAD - 2

        @pl.when((e >= 0) & (e < chunks) & is_odd & (lax.rem(e, 3) == 2))
        def _():
            passed(e).wait_recv()
            last(e).start()

        h = t - AHEAD - 3

        @pl.when((h >= 0) & (h < chunks))
        def _():
            first = pl.multiple_of(h * CHUNK, CHUNK)
            fetch = pltpu.make_async_copy(lower_hbm.at[pl.ds(first, CHUNK)], lower, lower_sem)
            fetch.start()
            second(h).wait_recv()
            fetch.wait()
            for k, held in enumerate((own, from_one, from_two, from_three)):
                totals[k] += lax.dot_general(
                    held[h], lower[...], (((0,), (0,)), ((), ())), preferred_element_type=jnp.float32
                )

        return carry

    lax.fori_loop(0, chunks + AHEAD + 3, body, 0)

    def drain(c, carry):
        kind = lax.rem(c, 3)
        up(c).wait_send()

        @pl.when(is_even)
        def _():
            across(c).wait_send()

        @pl.when(is_odd)
        def _():
            swap_odd(c).wait_send()

        @pl.when(is_odd & (kind == 2))
        def _():
            passed(c).wait_send()
            last(c).wait_send()

        @pl.when(is_even & (kind != 0))
        def _():
            swap_even(c).wait_send()

        @pl.when((kind == 0) | (is_even & (kind == 1)))
        def _():
            second(c).wait_send()

        return carry

    lax.fori_loop(0, chunks, drain, 0)
    share = totals.shape[1] // parts
    for p in range(parts):
        for k in range(STEPS):
            out[pl.ds((p * STEPS + k) * share, share), :] = totals[k, pl.ds(p * share, share), :]


def partial_moments(states, parts, offsets, low, high, upper_vectors, dipole_blocks, lower_vectors):
    rows, upper_count = upper_vectors.shape
    lower_count = lower_vectors.shape[1]
    block_size = dipole_blocks.shape[1]
    chunks = rows // CHUNK
    groups = (chunks + 2) // 3
    held = pltpu.VMEM((chunks, CHUNK, upper_count), jnp.bfloat16)
    vmem = pl.BlockSpec(memory_space=pltpu.VMEM)
    hbm = pl.BlockSpec(memory_space=pl.ANY)
    dma = pltpu.SemaphoreType.DMA
    return pl.pallas_call(
        functools.partial(kernel, states, parts, chunks, block_size),
        out_shape=jax.ShapeDtypeStruct((upper_count * STEPS, lower_count), jnp.float32),
        in_specs=[pl.BlockSpec(memory_space=pltpu.SMEM), vmem, vmem, hbm, vmem, hbm],
        out_specs=vmem,
        scratch_shapes=[
            pltpu.VMEM((rows // block_size + 4, block_size, upper_count), jnp.bfloat16),
            held,
            held,
            held,
            held,
            pltpu.VMEM((groups, CHUNK, upper_count), jnp.bfloat16),
            pltpu.VMEM((CHUNK, lower_count), jnp.bfloat16),
            pltpu.VMEM((STEPS, upper_count, lower_count), jnp.float32),
            dma,
            dma,
            dma((chunks,)),
            dma((chunks,)),
            dma((chunks,)),
            dma((groups,)),
            dma((chunks,)),
            dma((chunks,)),
            dma((chunks,)),
            dma((chunks,)),
            dma((groups,)),
            dma((groups,)),
        ],
        compiler_params=pltpu.CompilerParams(
            collective_id=0, has_side_effects=True, vmem_limit_bytes=58 * 1024 * 1024
        ),
        cost_estimate=pl.CostEstimate(
            flops=2 * rows * upper_count * (STEPS * lower_count + 2 * block_size),
            bytes_accessed=2 * rows * (upper_count + lower_count + 2 * block_size),
            transcendentals=0,
        ),
    )(
        offsets,
        low.reshape(2, block_size, upper_count),
        high.reshape(2, block_size, upper_count),
        upper_vectors.reshape(-1, block_size, upper_count),
        dipole_blocks,
        lower_vectors,
    )


def halos(block, width):
    count = lax.axis_size("basis")
    forward = [(i, i + 1) for i in range(count - 1)]
    backward = [(target, source) for source, target in forward]
    low = lax.ppermute(lax.slice_in_dim(block, block.shape[0] - width, None, axis=0), "basis", forward)
    high = lax.ppermute(lax.slice_in_dim(block, 0, width, axis=0), "basis", backward)
    return low, high


def window_labels(upper_labels):
    count = lax.axis_size("state")
    windows = [upper_labels]
    for k in range(1, STEPS):
        pairs = [(source, (source + k) % count) for source in range(count)]
        windows.append(lax.ppermute(upper_labels, "state", pairs))
    return jnp.stack(windows, axis=1).reshape(-1)


def local(
    lower_vectors,
    upper_vectors,
    lower_labels,
    upper_labels,
    band_offsets,
    dipole_blocks,
    pair_table,
):
    states = lax.axis_size("state")
    basis = lax.axis_size("basis")
    low, high = halos(upper_vectors, 2 * dipole_blocks.shape[1])
    partial = partial_moments(
        states, basis, band_offsets, low, high, upper_vectors, dipole_blocks, lower_vectors
    )
    summed = lax.psum_scatter(partial, "basis", scatter_dimension=0, tiled=True)
    labels = window_labels(upper_labels)
    share = labels.shape[0] // basis
    labels = lax.dynamic_slice_in_dim(labels, lax.axis_index("basis") * share, share, 0)
    symbols = jnp.arange(pair_table.shape[0], dtype=jnp.int32)
    lower_onehot = (lower_labels[:, None] == symbols[None, :]).astype(jnp.float32)
    upper_onehot = (labels[:, None] == symbols[None, :]).astype(jnp.float32)
    allowed = jnp.dot(
        jnp.dot(lower_onehot, pair_table.astype(jnp.float32), precision=lax.Precision.HIGHEST),
        upper_onehot.T,
        precision=lax.Precision.HIGHEST,
    )
    norm_scale = float(lower_vectors.shape[0] * basis) ** (-0.5)
    summed = summed.reshape(STEPS, -1, summed.shape[1]).transpose(2, 1, 0)
    return summed.reshape(allowed.shape) * allowed * norm_scale


def solution(mesh):
    return jax.shard_map(
        local,
        mesh=mesh,
        in_specs=(
            P("basis", "state"),
            P("basis", "state"),
            P("state"),
            P("state"),
            P("basis"),
            P("basis", None, None),
            P(),
        ),
        out_specs=P("state", "basis"),
        check_vma=False,
    )
```

time: 663 us -> 353 us (0.53)
  waiting for transfers between devices: 559 us -> 26.3 us
  Pallas kernels: 0 us -> 302 us
  matrix products: 42.2 us -> 1.44 us
  other arithmetic: 25.7 us -> 0.01 us
  local copies, waits for them, and re-layouts: 17.4 us -> 3.4 us
    ppermute x8 -> x5, waiting for transfers between devices: 535 us -> 7.58 us  [the longest x1 3.96 us: halos(): lax.ppermute(lax.slice_in_dim(block, 0, width, axis=0), 'basis', backward)]
    pallas_call x0 -> x1, Pallas kernels: none -> 302 us  [partial_moments(): pl.pallas_call(functools.partial(kernel, states, parts, chunks, block_siz...]
    dot_general x10 -> x2, matrix products: 42.2 us -> 1.44 us  [the longest x1 1.15 us: local(): jnp.dot(jnp.dot(lower_onehot, pair_table.astype(jnp.float32), precision=l...]
    concatenate x1 -> x0, other arithmetic: 17.7 us -> none  [with_halo(): block = jnp.concatenate([low, block, high], axis=dim)]
    gather x1 -> x0, local copies, waits for them, and re-layouts: 11.8 us -> none  [local(): coupled = jnp.take(blocks, source_rows, axis=0)]
    select_n x1 -> x0, other arithmetic: 7.16 us -> none  [local(): coupled = jnp.take(blocks, source_rows, axis=0)]
  transfers between devices with their start and end apart: 9 -> 6, of which waited for: 7 -> 5; matrix products, arithmetic and copies ran while one was open for 4% -> 0% of each run, Pallas kernels for 0% -> 0%
where the time goes in v1:
time: 353 us; the launch traced here: 352 us
  Pallas kernels  302 us (86%)
  waiting for transfers between devices  26.3 us (7%)
  between operations  13.5 us (4%)
  starting transfers between devices  6.17 us (2%)
    pallas_call x1, Pallas kernels, partial_moments(): pl.pallas_call(functools.partial(kernel, states, parts, chunks, block_siz...  302 us
    reduce_scatter x1, waiting for transfers between devices, local(): summed = lax.psum_scatter(partial, 'basis', scatter_dimension=0, tiled=True)  18.7 us
  transfers between devices with their start and end apart: 6, of which 5 were waited for; matrix products, arithmetic and copies ran while one was open for 0% of the time, Pallas kernels for 0%

profile of v1, /device:TPU:0, one launch (start us, length us, event | category | flops | bytes accessed | tf_op | source)
XLA Modules:
  0.0 352.3 jit_solution(11018407706421526806)
XLA Ops:
  6.5 0.0 reduce-scatter.2.cloned.1.call-start
  6.5 0.9 fusion.5
  7.4 2.4 collective-permute-start
  9.8 1.3 collective-permute-start.1
  11.1 0.0 collective-permute-done
  11.1 0.0 copy-start.3
  11.1 4.0 %collective-permute-done.1 = bf16[128,256]{1,0:T(8,128)(2,1)S(1)} collective-permute-done((bf16[128,256]{1,0:T(8,128)(2,1)S(1)}, bf16[128,256]{1,0:T(8,128)(2,1)S(1)}, u32[]{:S(2)}, u32[]{:S(2)}) %collective-permute-start.1) | collective-permute-done | bytes 65568 | tf_op jit(solution)/shard_map/ppermute | solution.py:269
  15.1 0.0 copy-start.4
  15.1 0.0 copy-done.3
  15.1 0.6 copy-done.4
  15.7 0.0 copy-start.2
  15.7 0.0 copy-start
  15.7 0.0 copy-start.1
  15.7 301.5 %shard_map.73 = f32[1024,384]{1,0:T(8,128)} custom-call(s32[240]{0:T(256)} %offsets.1, bf16[2,64,256]{2,1,0:T(8,128)(2,1)} %bitcast.21, bf16[2,64,256]{2,1,0:T(8,128)(2,1)} %bitcast.22, bf16[240,64,256]{2,1,0:T(8,128)(2,1)} %bitcast.16, bf16[240,64,128]{2,1,0:T(8,128)(2,1)} %dipole.1, bf16[15360,384]{1,0:T(8,128)(2,1)} %lower_hbm.1), custom_call_target="tpu_custom_call" | custom-call | flops 13086228480 | bytes 23592960 | tf_op jit(solution)/shard_map/pallas_call | solution.py:219
  317.2 0.0 reduce-scatter.2.cloned.1.call-update
  317.2 0.0 copy-done.2
  317.2 0.1 collective-permute-start.4
  317.3 0.1 collective-permute-start.3
  317.4 2.4 collective-permute-start.2
  319.8 0.0 copy-done
  319.8 0.0 copy-done.1
  319.8 0.3 fusion.1
  320.1 2.6 collective-permute-done.4
  322.7 0.1 collective-permute-done.3
  322.7 1.0 collective-permute-done.2
  323.7 0.1 copy.10
  323.9 0.1 reshape.25
  324.0 0.1 dynamic_slice.3
  324.1 18.7 %reduce-scatter.2.cloned.1.call-done = f32[256,384]{1,0:T(8,128)} async-done(((f32[1024,384]{1,0:T(8,128)}), f32[256,384]{1,0:T(8,128)}) %reduce-scatter.2.cloned.1.call-update) | async-done | bytes 393232 | tf_op jit(solution)/shard_map/reduce_scatter | solution.py:297
  342.7 1.3 copy.13
  344.0 0.1 reshape.24
  344.1 0.2 copy.11
  344.3 1.2 fusion
  (1 shorter events, 0.0 us)
Async XLA Ops:
  6.5 336.2 %reduce-scatter.2.cloned.1.call-start = ((), (), s32[]{:S(2)}) async-start(), calls=%async_computation.1 | async-start | bytes 1966080 | tf_op jit(solution)/shard_map/reduce_scatter | solution.py:297
  7.4 3.7 %collective-permute-start = (bf16[128,256]{1,0:T(8,128)(2,1)S(1)}, bf16[128,256]{1,0:T(8,128)(2,1)S(1)}, u32[]{:S(2)}, u32[]{:S(2)}) collective-permute-start(bf16[128,256]{1,0:T(8,128)(2,1)S(1)} %get-tuple-element.6), channel_id=1, source_target_pairs={{0,1},{1,2},{2,3},{4,5},{5,6},{6,7},{8,9},{9,10},{10,11},{12,13},{... | collective-permute-start | bytes 196616 | tf_op jit(solution)/shard_map/ppermute | solution.py:268
  9.8 5.3 %collective-permute-start.1 = (bf16[128,256]{1,0:T(8,128)(2,1)S(1)}, bf16[128,256]{1,0:T(8,128)(2,1)S(1)}, u32[]{:S(2)}, u32[]{:S(2)}) collective-permute-start(bf16[128,256]{1,0:T(8,128)(2,1)S(1)} %get-tuple-element.5), channel_id=1, source_target_pairs={{1,0},{2,1},{3,2},{5,4},{6,5},{7,6},{9,8},{10,9},{11,10},{13,12},{... | collective-permute-start | bytes 196616 | tf_op jit(solution)/shard_map/ppermute | solution.py:269
  11.1 4.0 %copy-start.3 = (bf16[128,256]{1,0:T(8,128)(2,1)}, bf16[128,256]{1,0:T(8,128)(2,1)S(1)}, u32[]{:S(2)}) copy-start(bf16[128,256]{1,0:T(8,128)(2,1)S(1)} %collective-permute-done) | copy-start | bytes 196612
  15.1 0.6 copy-start.4
  15.7 301.6 %copy-start.2 = (s32[256]{0:T(256)S(1)}, s32[256]{0:T(256)}, u32[]{:S(2)}) copy-start(s32[256]{0:T(256)} %param.10) | copy-start | bytes 3076
  15.7 304.1 %copy-start = (s32[384]{0:T(512)S(1)}, s32[384]{0:T(512)}, u32[]{:S(2)}) copy-start(s32[384]{0:T(512)} %param.9) | copy-start | bytes 4612
  15.7 304.1 %copy-start.1 = (s32[4,4]{1,0:T(4,128)S(1)}, s32[4,4]{1,0:T(4,128)}, u32[]{:S(2)}) copy-start(s32[4,4]{1,0:T(4,128)} %param.13) | copy-start | bytes 196
  317.2 5.4 %collective-permute-start.4 = (s32[256]{0:T(256)S(1)}, s32[256]{0:T(256)S(1)}, u32[]{:S(2)}, u32[]{:S(2)}) collective-permute-start(s32[256]{0:T(256)S(1)} %copy-done.2), channel_id=1, source_target_pairs={{0,12},{4,16},{8,20},{12,24},{16,28},{20,0},{24,4},{28,8},{1,13},{... | collective-permute-start | bytes 3080 | tf_op jit(solution)/shard_map/ppermute | solution.py:278
  317.3 5.4 %collective-permute-start.3 = (s32[256]{0:T(256)S(1)}, s32[256]{0:T(256)S(1)}, u32[]{:S(2)}, u32[]{:S(2)}) collective-permute-start(s32[256]{0:T(256)S(1)} %copy-done.2), channel_id=1, source_target_pairs={{0,8},{4,12},{8,16},{12,20},{16,24},{20,28},{24,0},{28,4},{1,9},{5... | collective-permute-start | bytes 3080 | tf_op jit(solution)/shard_map/ppermute | solution.py:278
  317.4 6.3 %collective-permute-start.2 = (s32[256]{0:T(256)S(1)}, s32[256]{0:T(256)S(1)}, u32[]{:S(2)}, u32[]{:S(2)}) collective-permute-start(s32[256]{0:T(256)S(1)} %copy-done.2), channel_id=1, source_target_pairs={{0,4},{4,8},{8,12},{12,16},{16,20},{20,24},{24,28},{28,0},{1,5},{5... | collective-permute-start | bytes 3080 | tf_op jit(solution)/shard_map/ppermute | solution.py:278
Sparse Core Ops, SparseCore 0:
  317.4 25.3 reduce-scatter.1

commit v2 on v1

--- a/solution.py
+++ b/solution.py
@@ -9,7 +9,7 @@
 
 STEPS = 4
 CHUNK = 512
-AHEAD = 3
+AHEAD = 2
 MESH = pl.DeviceIdType.MESH
 
 
@@ -19,12 +19,12 @@
     chunks,
     block_size,
     offsets,
-    low,
-    high,
+    labels,
     upper_hbm,
     dipole,
     lower_hbm,
     out,
+    labels_out,
     upper,
     own,
     from_two,
@@ -45,6 +45,17 @@
     send_second,
     send_passing,
     send_last,
+    windows,
+    near,
+    far,
+    label_send,
+    label_sem,
+    halo_send,
+    halo_sem,
+    near_send,
+    near_sem,
+    far_send,
+    far_sem,
 ):
     me = lax.axis_index("state")
     odd = lax.rem(me, 2)
@@ -56,16 +67,65 @@
     blocks = upper_hbm.shape[0]
     per_chunk = CHUNK // block_size
 
+    part = lax.axis_index("basis")
+    core = lax.rem(part, 2)
+    place = part // 2
+    places = parts // 2
+
     load = pltpu.make_async_copy(upper_hbm, upper.at[pl.ds(2, blocks)], load_sem)
     load.start()
     barrier = pltpu.get_barrier_semaphore()
-    for other in (partner, above, below):
-        pl.semaphore_signal(barrier, inc=1, device_id={"state": other}, device_id_type=MESH)
-    upper[pl.ds(0, 2)] = low[...]
-    upper[pl.ds(2 + blocks, 2)] = high[...]
+    for step in range(1, STEPS):
+        for other in (lax.rem(me + step, states), lax.rem(me + states - step, states)):
+            pl.semaphore_signal(barrier, inc=1, device_id={"state": other}, device_id_type=MESH)
+    for step in range(1, parts):
+        other = lax.rem(part + step, parts)
+        pl.semaphore_signal(barrier, inc=1, device_id={"basis": other}, device_id_type=MESH)
+    edge = jnp.zeros((2,) + upper.shape[1:], upper.dtype)
+
+    @pl.when(part == 0)
+    def _():
+        upper[pl.ds(0, 2)] = edge
+
+    @pl.when(part == parts - 1)
+    def _():
+        upper[pl.ds(2 + blocks, 2)] = edge
+
     totals[...] = jnp.zeros_like(totals)
-    load.wait()
-    pl.semaphore_wait(barrier, 3)
+    pl.semaphore_wait(barrier, 2 * (STEPS - 1) + parts - 1)
+
+    def along(source, target, send, receive, device):
+        return pltpu.make_async_remote_copy(
+            src_ref=source,
+            dst_ref=target,
+            send_sem=send,
+            recv_sem=receive,
+            device_id={"basis": device},
+            device_id_type=MESH,
+        )
+
+    to_next = along(
+        upper_hbm.at[pl.ds(blocks - 2, 2)],
+        upper.at[pl.ds(0, 2)],
+        halo_send.at[0],
+        halo_sem.at[0],
+        lax.rem(part + 1, parts),
+    )
+    to_last = along(
+        upper_hbm.at[pl.ds(0, 2)],
+        upper.at[pl.ds(2 + blocks, 2)],
+        halo_send.at[1],
+        halo_sem.at[1],
+        lax.rem(part + parts - 1, parts),
+    )
+
+    @pl.when(part < parts - 1)
+    def _():
+        to_next.start()
+
+    @pl.when(part > 0)
+    def _():
+        to_last.start()
 
     def copy(source, target, send, receive, device):
         return pltpu.make_async_remote_copy(
@@ -77,6 +137,62 @@
             device_id_type=MESH,
         )
 
+    def window(k):
+        return copy(
+            labels,
+            windows.at[k - 1],
+            label_send.at[k - 1],
+            label_sem.at[k - 1],
+            lax.rem(me + k, states),
+        )
+
+    for k in range(1, STEPS):
+        window(k).start()
+    load.wait()
+
+    @pl.when(part > 0)
+    def _():
+        to_next.wait_recv()
+
+    @pl.when(part < parts - 1)
+    def _():
+        to_last.wait_recv()
+
+    def near_copy(k):
+        return along(
+            totals.at[k, :, 1 - core],
+            near.at[k],
+            near_send.at[k],
+            near_sem.at[k],
+            part + 1 - 2 * core,
+        )
+
+    def far_copy(k, d):
+        target = lax.rem(place + d, places)
+        return along(
+            near.at[k, target],
+            far.at[k, d - 1],
+            far_send.at[k, d - 1],
+            far_sem.at[k, d - 1],
+            target * 2 + core,
+        )
+
+    def pair_sum(k):
+        near_copy(k).wait_recv()
+        near[k] += totals[k, :, core]
+        for d in range(1, places):
+            far_copy(k, d).start()
+
+    def add_product(k, held):
+        product = lax.dot_general(
+            held, lower[...], (((0,), (0,)), ((), ())), preferred_element_type=jnp.float32
+        )
+        totals[k] += product.reshape(totals.shape[1:])
+
+    def fetch(c):
+        first = pl.multiple_of(c * CHUNK, CHUNK)
+        return pltpu.make_async_copy(lower_hbm.at[pl.ds(first, CHUNK)], lower, lower_sem)
+
     def up(c):
         return copy(own.at[c], from_two.at[c], send_up.at[c], two_sem.at[c], above)
 
@@ -147,6 +263,22 @@
             def _():
                 second(b).start()
 
+            fetch(b).start()
+            fetch(b).wait()
+            add_product(0, own[b])
+            add_product(1, from_one[b])
+            add_product(2, from_two[b])
+
+        @pl.when(b == chunks - 1)
+        def _():
+            for k in range(STEPS - 1):
+                near_copy(k).start()
+
+        @pl.when(b == chunks)
+        def _():
+            for k in range(STEPS - 1):
+                pair_sum(k)
+
         e = t - AHEAD - 2
 
         @pl.when((e >= 0) & (e < chunks) & is_odd & (lax.rem(e, 3) == 2))
@@ -158,19 +290,16 @@
 
         @pl.when((h >= 0) & (h < chunks))
         def _():
-            first = pl.multiple_of(h * CHUNK, CHUNK)
-            fetch = pltpu.make_async_copy(lower_hbm.at[pl.ds(first, CHUNK)], lower, lower_sem)
-            fetch.start()
+            fetch(h).start()
             second(h).wait_recv()
-            fetch.wait()
-            for k, held in enumerate((own, from_one, from_two, from_three)):
-                totals[k] += lax.dot_general(
-                    held[h], lower[...], (((0,), (0,)), ((), ())), preferred_element_type=jnp.float32
-                )
+            fetch(h).wait()
+            add_product(3, from_three[h])
 
         return carry
 
     lax.fori_loop(0, chunks + AHEAD + 3, body, 0)
+    near_copy(STEPS - 1).start()
+    pair_sum(STEPS - 1)
 
     def drain(c, carry):
         kind = lax.rem(c, 3)
@@ -200,27 +329,49 @@
         return carry
 
     lax.fori_loop(0, chunks, drain, 0)
-    share = totals.shape[1] // parts
-    for p in range(parts):
-        for k in range(STEPS):
-            out[pl.ds((p * STEPS + k) * share, share), :] = totals[k, pl.ds(p * share, share), :]
-
-
-def partial_moments(states, parts, offsets, low, high, upper_vectors, dipole_blocks, lower_vectors):
+
+    @pl.when(part < parts - 1)
+    def _():
+        to_next.wait_send()
+
+    @pl.when(part > 0)
+    def _():
+        to_last.wait_send()
+
+    labels_out[0] = labels[...]
+    for k in range(1, STEPS):
+        window(k).wait()
+        labels_out[k] = windows[k - 1]
+    for k in range(STEPS):
+        near_copy(k).wait_send()
+        total = near[k, place]
+        for d in range(1, places):
+            far_copy(k, d).wait()
+            total = total + far[k, d - 1]
+        out[k] = total
+
+
+def moment_sums(states, parts, offsets, labels, upper_vectors, dipole_blocks, lower_vectors):
     rows, upper_count = upper_vectors.shape
     lower_count = lower_vectors.shape[1]
     block_size = dipole_blocks.shape[1]
     chunks = rows // CHUNK
     groups = (chunks + 2) // 3
+    share = upper_count // parts
+    places = parts // 2
+    labels = jnp.broadcast_to(labels[None, :], (8, upper_count))
     held = pltpu.VMEM((chunks, CHUNK, upper_count), jnp.bfloat16)
     vmem = pl.BlockSpec(memory_space=pltpu.VMEM)
     hbm = pl.BlockSpec(memory_space=pl.ANY)
     dma = pltpu.SemaphoreType.DMA
     return pl.pallas_call(
         functools.partial(kernel, states, parts, chunks, block_size),
-        out_shape=jax.ShapeDtypeStruct((upper_count * STEPS, lower_count), jnp.float32),
-        in_specs=[pl.BlockSpec(memory_space=pltpu.SMEM), vmem, vmem, hbm, vmem, hbm],
-        out_specs=vmem,
+        out_shape=(
+            jax.ShapeDtypeStruct((STEPS, share, lower_count), jnp.float32),
+            jax.ShapeDtypeStruct((STEPS, 8, upper_count), jnp.int32),
+        ),
+        in_specs=[pl.BlockSpec(memory_space=pltpu.SMEM), vmem, hbm, vmem, hbm],
+        out_specs=(vmem, vmem),
         scratch_shapes=[
             pltpu.VMEM((rows // block_size + 4, block_size, upper_count), jnp.bfloat16),
             held,
@@ -229,7 +380,7 @@
             held,
             pltpu.VMEM((groups, CHUNK, upper_count), jnp.bfloat16),
             pltpu.VMEM((CHUNK, lower_count), jnp.bfloat16),
-            pltpu.VMEM((STEPS, upper_count, lower_count), jnp.float32),
+            pltpu.VMEM((STEPS, places, 2, share, lower_count), jnp.float32),
             dma,
             dma,
             dma((chunks,)),
@@ -242,6 +393,17 @@
             dma((chunks,)),
             dma((groups,)),
             dma((groups,)),
+            pltpu.VMEM((STEPS - 1, 8, upper_count), jnp.int32),
+            pltpu.VMEM((STEPS, places, share, lower_count), jnp.float32),
+            pltpu.VMEM((STEPS, places - 1, share, lower_count), jnp.float32),
+            dma((STEPS - 1,)),
+            dma((STEPS - 1,)),
+            dma((2,)),
+            dma((2,)),
+            dma((STEPS,)),
+            dma((STEPS,)),
+            dma((STEPS, places - 1)),
+            dma((STEPS, places - 1)),
         ],
         compiler_params=pltpu.CompilerParams(
             collective_id=0, has_side_effects=True, vmem_limit_bytes=58 * 1024 * 1024
@@ -253,30 +415,11 @@
         ),
     )(
         offsets,
-        low.reshape(2, block_size, upper_count),
-        high.reshape(2, block_size, upper_count),
+        labels,
         upper_vectors.reshape(-1, block_size, upper_count),
         dipole_blocks,
         lower_vectors,
     )
-
-
-def halos(block, width):
-    count = lax.axis_size("basis")
-    forward = [(i, i + 1) for i in range(count - 1)]
-    backward = [(target, source) for source, target in forward]
-    low = lax.ppermute(lax.slice_in_dim(block, block.shape[0] - width, None, axis=0), "basis", forward)
-    high = lax.ppermute(lax.slice_in_dim(block, 0, width, axis=0), "basis", backward)
-    return low, high
-
-
-def window_labels(upper_labels):
-    count = lax.axis_size("state")
-    windows = [upper_labels]
-    for k in range(1, STEPS):
-        pairs = [(source, (source + k) % count) for source in range(count)]
-        windows.append(lax.ppermute(upper_labels, "state", pairs))
-    return jnp.stack(windows, axis=1).reshape(-1)
 
 
 def local(
@@ -290,12 +433,10 @@
 ):
     states = lax.axis_size("state")
     basis = lax.axis_size("basis")
-    low, high = halos(upper_vectors, 2 * dipole_blocks.shape[1])
-    partial = partial_moments(
-        states, basis, band_offsets, low, high, upper_vectors, dipole_blocks, lower_vectors
-    )
-    summed = lax.psum_scatter(partial, "basis", scatter_dimension=0, tiled=True)
-    labels = window_labels(upper_labels)
+    summed, windows = moment_sums(
+        states, basis, band_offsets, upper_labels, upper_vectors, dipole_blocks, lower_vectors
+    )
+    labels = windows[:, 0, :].T.reshape(-1)
     share = labels.shape[0] // basis
     labels = lax.dynamic_slice_in_dim(labels, lax.axis_index("basis") * share, share, 0)
     symbols = jnp.arange(pair_table.shape[0], dtype=jnp.int32)
@@ -307,7 +448,7 @@
         precision=lax.Precision.HIGHEST,
     )
     norm_scale = float(lower_vectors.shape[0] * basis) ** (-0.5)
-    summed = summed.reshape(STEPS, -1, summed.shape[1]).transpose(2, 1, 0)
+    summed = summed.transpose(2, 1, 0)
     return summed.reshape(allowed.shape) * allowed * norm_scale
 
 

time: 353 us -> 316 us (0.90)
  waiting for transfers between devices: 26.3 us -> 0 us
  between operations: 13.5 us -> 0.07 us
  starting transfers between devices: 6.17 us -> 0 us
  Pallas kernels: 302 us -> 308 us
    reduce_scatter x1 -> x0, waiting for transfers between devices: 18.7 us -> none  [local(): summed = lax.psum_scatter(partial, 'basis', scatter_dimension=0, tiled=True)]
    ppermute x5 -> x0, waiting for transfers between devices: 7.58 us -> none  [the longest x1 3.96 us: halos(): lax.ppermute(lax.slice_in_dim(block, 0, width, axis=0), 'basis', backward)]
    pallas_call x1, Pallas kernels: 302 us -> 308 us  [moment_sums(): pl.pallas_call(functools.partial(kernel, states, parts, chunks, block_siz...]
    ppermute x5 -> x0, starting transfers between devices: 6.16 us -> none  [the longest x3 2.51 us: window_labels(): windows.append(lax.ppermute(upper_labels, 'state', pairs))]
  transfers between devices with their start and end apart: 6 -> 0, of which waited for: 5 -> 0; matrix products, arithmetic and copies ran while one was open for 0% -> 0% of each run, Pallas kernels for 0% -> 0%
where the time goes in v2:
time: 316 us; the launch traced here: 314 us
  Pallas kernels  308 us (97%)
  local copies, waits for them, and re-layouts  3.94 us (1%)
    pallas_call x1, Pallas kernels, moment_sums(): pl.pallas_call(functools.partial(kernel, states, parts, chunks, block_siz...  308 us

profile of v2, /device:TPU:0, one launch (start us, length us, event | category | flops | bytes accessed | tf_op | source)
XLA Modules:
  0.0 313.8 jit_solution(16296213132993978706)
XLA Ops:
  0.0 1.3 broadcast_in_dim.2.labels
  1.3 0.0 copy-start
  1.3 0.0 copy-start.1
  1.3 308.3 %shard_map.73 = (f32[4,64,384]{2,1,0:T(8,128)}, s32[4,8,256]{2,1,0:T(8,128)}) custom-call(s32[240]{0:T(256)} %offsets.1, s32[8,256]{1,0:T(8,128)} %broadcast_in_dim.2.labels, bf16[240,64,256]{2,1,0:T(8,128)(2,1)} %bitcast.12, bf16[240,64,128]{2,1,0:T(8,128)(2,1)} %dipole.1, bf16[15360,384]{1,0:T(8,128)(2,1)} %lower_hbm.1), custom_call_target="tpu_custom_call" | custom-call | flops 13086228480 | bytes 23592960 | tf_op jit(solution)/shard_map/pallas_call | solution.py:367
  309.6 0.8 slice.3
  310.4 0.1 copy.9
  310.5 0.1 reshape.14
  310.6 0.1 dynamic_slice.3
  310.7 1.3 copy.8
  312.0 0.1 reshape.13
  312.1 0.2 copy.10
  312.3 0.0 copy-done
  312.3 0.0 copy-done.1
  312.3 0.3 fusion.1
  312.6 1.2 fusion
  (1 shorter events, 0.0 us)
Async XLA Ops:
  1.3 311.0 %copy-start = (s32[384]{0:T(512)S(1)}, s32[384]{0:T(512)}, u32[]{:S(2)}) copy-start(s32[384]{0:T(512)} %param.9) | copy-start | bytes 4612
  1.3 311.0 %copy-start.1 = (s32[4,4]{1,0:T(4,128)S(1)}, s32[4,4]{1,0:T(4,128)}, u32[]{:S(2)}) copy-start(s32[4,4]{1,0:T(4,128)} %param.13) | copy-start | bytes 196

commit v3 on v2

--- a/solution.py
+++ b/solution.py
@@ -8,8 +8,9 @@
 from jax.sharding import PartitionSpec as P
 
 STEPS = 4
-CHUNK = 512
+CHUNK = 384
 AHEAD = 2
+LAGS = (1, 2, 4)
 MESH = pl.DeviceIdType.MESH
 
 
@@ -252,7 +253,7 @@
             def _():
                 swap_even(c).start()
 
-        b = t - AHEAD - 1
+        b = t - AHEAD - LAGS[0]
 
         @pl.when((b >= 0) & (b < chunks))
         def _():
@@ -279,14 +280,14 @@
             for k in range(STEPS - 1):
                 pair_sum(k)
 
-        e = t - AHEAD - 2
+        e = t - AHEAD - LAGS[1]
 
         @pl.when((e >= 0) & (e < chunks) & is_odd & (lax.rem(e, 3) == 2))
         def _():
             passed(e).wait_recv()
             last(e).start()
 
-        h = t - AHEAD - 3
+        h = t - AHEAD - LAGS[2]
 
         @pl.when((h >= 0) & (h < chunks))
         def _():
@@ -297,7 +298,7 @@
 
         return carry
 
-    lax.fori_loop(0, chunks + AHEAD + 3, body, 0)
+    lax.fori_loop(0, chunks + AHEAD + max(LAGS[2], LAGS[0] + 1), body, 0)
     near_copy(STEPS - 1).start()
     pair_sum(STEPS - 1)
 

time: 316 us -> 315 us (level)
  no operation moved by 1% of the time
where the time goes in v3:
time: 315 us; the launch traced here: 312 us
  Pallas kernels  306 us (97%)
  local copies, waits for them, and re-layouts  3.94 us (1%)
    pallas_call x1, Pallas kernels, moment_sums(): pl.pallas_call(functools.partial(kernel, states, parts, chunks, block_siz...  306 us

profile of v3, /device:TPU:0, one launch (start us, length us, event | category | flops | bytes accessed | tf_op | source)
XLA Modules:
  0.0 311.8 jit_solution(9029801569392605861)
XLA Ops:
  0.0 1.3 broadcast_in_dim.2.labels
  1.3 0.0 copy-start
  1.3 0.0 copy-start.1
  1.3 306.3 %shard_map.73 = (f32[4,64,384]{2,1,0:T(8,128)}, s32[4,8,256]{2,1,0:T(8,128)}) custom-call(s32[240]{0:T(256)} %offsets.1, s32[8,256]{1,0:T(8,128)} %broadcast_in_dim.2.labels, bf16[240,64,256]{2,1,0:T(8,128)(2,1)} %bitcast.12, bf16[240,64,128]{2,1,0:T(8,128)(2,1)} %dipole.1, bf16[15360,384]{1,0:T(8,128)(2,1)} %lower_hbm.1), custom_call_target="tpu_custom_call" | custom-call | flops 13086228480 | bytes 23592960 | tf_op jit(solution)/shard_map/pallas_call | solution.py:368
  307.6 0.8 slice.3
  308.4 0.1 copy.9
  308.5 0.1 reshape.14
  308.6 0.1 dynamic_slice.3
  308.7 1.3 copy.8
  310.0 0.1 reshape.13
  310.1 0.2 copy.10
  310.3 0.0 copy-done
  310.3 0.0 copy-done.1
  310.3 0.3 fusion.1
  310.6 1.2 fusion
  (1 shorter events, 0.0 us)
Async XLA Ops:
  1.3 309.0 %copy-start = (s32[384]{0:T(512)S(1)}, s32[384]{0:T(512)}, u32[]{:S(2)}) copy-start(s32[384]{0:T(512)} %param.9) | copy-start | bytes 4612
  1.3 309.0 %copy-start.1 = (s32[4,4]{1,0:T(4,128)S(1)}, s32[4,4]{1,0:T(4,128)}, u32[]{:S(2)}) copy-start(s32[4,4]{1,0:T(4,128)} %param.13) | copy-start | bytes 196
